TPU v7x, 32 devices: a whole 2x2x4 slice. The times are simulated.
32 devices in a mesh: groups: 2 (over y), store: 16 (over z, x, core).
Axes of the slice: x: 2, y: 2, z: 4, core: 2. Of those that a mesh axis runs over, the one named last changes fastest.
Arguments:
- layer_input: bfloat16 [12288, 8192], P('groups', 'store'), parts along dimension 0, may hold values from -6 to 6
- output_grad: bfloat16 [12288, 8192], P('groups', 'store'), parts along dimension 0, may hold values from -6 to 6
- proj_in: bfloat16 [8192, 64], P('store'), may hold values from -0.0625 to 0.0625
- proj_out: bfloat16 [8192, 64], P('store'), may hold values from -0.0625 to 0.0625
- precond_in: float32 [64, 64], replicated
- precond_out: float32 [64, 64], replicated
- query_lengths: int32 [768], P('groups'), parts along dimension 0, may hold values from 1 to 16
- store_rows: bfloat16 [8192, 4096], P('store'), may hold values from -0.0234375 to 0.0234375
- store_live: int32 [16], P('store'), may hold values from 256 to 512, as said below
Outputs:
- scores: float32 [768, 8192], P('groups', 'store'), parts along dimension 0
There are 2 independent parts, one for each index of `groups`. A program takes and returns all parts, laid end to end along the dimension named above; an argument that names none is the same for every part. Nothing has to cross between parts.
Inputs may be any that keep to these rules, and one draw needn't show every extreme that they name: Shard k of the store holds store_live[k] live rows at its head; some shard is full.
All inputs are finite; a program needn't handle non-finite values.
Results may differ from a plain program's by a relative error of at most 0.0029.
Values may be sent and summed in bfloat16 or wider, within the bound.
A program may use at most 128 MiB of HBM per device.

v0:
```python
import jax
import jax.numpy as jnp
from jax import lax
from jax.sharding import PartitionSpec as P


def project_pair(input_rows, grad_rows, weight_in, weight_out):
    return jnp.concatenate(
        [
            jnp.dot(input_rows, weight_in, preferred_element_type=jnp.float32),
            jnp.dot(grad_rows, weight_out, preferred_element_type=jnp.float32),
        ],
        axis=1,
    )


def precondition(factors, lengths, precond_in, precond_out):
    query_count = lengths.shape[0]
    proj_rank = precond_in.shape[0]
    query_len = factors.shape[0] // query_count
    token_keep = (jnp.arange(query_len, dtype=jnp.int32)[None, :] < lengths[:, None]).astype(
        jnp.float32
    )
    input_side = (
        factors[:, :proj_rank].reshape(query_count, query_len, proj_rank) * token_keep[:, :, None]
    )
    output_side = factors[:, proj_rank:].reshape(query_count, query_len, proj_rank)
    outer_sums = jnp.einsum(
        "qti,qtj->qij", input_side, output_side, precision=lax.Precision.HIGHEST
    )
    left_side = jnp.einsum("ai,qij->qaj", precond_in, outer_sums, precision=lax.Precision.HIGHEST)
    conditioned = jnp.einsum("qaj,jb->qab", left_side, precond_out, precision=lax.Precision.HIGHEST)
    return conditioned.reshape(query_count, proj_rank * proj_rank).astype(jnp.bfloat16)


def score_block(query_grads, store_rows, live_rows):
    products = lax.dot_general(
        query_grads, store_rows, (((1,), (1,)), ((), ())), preferred_element_type=jnp.float32
    )
    row_index = jnp.arange(store_rows.shape[0], dtype=jnp.int32)
    return jnp.where(row_index[None, :] < live_rows, products, 0.0)


def local(
    layer_input,
    output_grad,
    proj_in,
    proj_out,
    precond_in,
    precond_out,
    query_lengths,
    store_rows,
    store_live,
):
    live_rows = store_live[0]
    query_count = query_lengths.shape[0] // lax.axis_size("store")
    first_query = lax.axis_index("store") * query_count
    my_lengths = lax.dynamic_slice_in_dim(query_lengths, first_query, query_count, 0)
    factors = lax.psum_scatter(
        project_pair(layer_input, output_grad, proj_in, proj_out),
        "store",
        scatter_dimension=0,
        tiled=True,
    )
    query_grads = precondition(factors, my_lengths, precond_in, precond_out)
    return score_block(
        lax.all_gather(query_grads, "store", axis=0, tiled=True), store_rows, live_rows
    )


def solution(mesh):
    placed = (
        P("groups", "store"),
        P("groups", "store"),
        P("store", None),
        P("store", None),
        P(),
        P(),
        P("groups"),
        P("store", None),
        P("store"),
    )
    return jax.shard_map(
        local, mesh=mesh, in_specs=placed, out_specs=P("groups", "store"), check_vma=False
    )
```

profile of v0, /device:TPU:0, one launch (start us, length us, event | category | flops | bytes accessed | tf_op | source)
XLA Modules:
  0.0 147.7 jit_solution(9821974705541075636)
XLA Ops:
  6.5 0.0 copy-start
  6.5 0.0 reduce-scatter.2.cloned.1.call-start
  6.5 0.8 copy-done
  7.4 4.9 %fusion.8 = f32[6144,64]{0,1:T(8,128)S(1)} fusion(bf16[6144,512]{1,0:T(8,128)(2,1)} %param.10, bf16[512,64]{0,1:T(8,128)(2,1)S(1)} %copy-done), kind=kOutput, calls=%fused_computation.14 | convolution fusion | flops 402653184 | bytes 7929856 | tf_op jit(solution)/shard_map/dot_general | solution.py:11
  12.3 0.0 copy-done.2
  12.3 0.0 copy-done.1
  12.3 2.0 %fusion.7 = f32[6144,64]{0,1:T(8,128)S(1)} fusion(bf16[6144,512]{1,0:T(8,128)(2,1)S(1)} %copy-done.1, bf16[512,64]{0,1:T(8,128)(2,1)S(1)} %copy-done.2), kind=kOutput, calls=%fused_computation.13 | convolution fusion | flops 402653184 | bytes 7929856 | tf_op jit(solution)/shard_map/dot_general | solution.py:10
  14.3 1.9 %pad_maximum_fusion = f32[6144,128]{0,1:T(8,128)} fusion(f32[6144,64]{0,1:T(8,128)S(1)} %fusion.8, f32[6144,64]{0,1:T(8,128)S(1)} %fusion.7), kind=kLoop, calls=%fused_computation | loop fusion | flops 786432 | bytes 6291456 | tf_op jit(solution)/shard_map/concatenate | solution.py:8
  16.2 0.0 reduce-scatter.2.cloned.1.call-update
  16.2 0.0 all-gather.2.cloned.1.call-start
  16.3 0.8 dynamic_slice.3
  17.1 0.1 fusion.5
  17.1 68.2 %reduce-scatter.2.cloned.1.call-done = f32[384,128]{0,1:T(8,128)} async-done(((f32[6144,128]{0,1:T(8,128)}), f32[384,128]{0,1:T(8,128)}) %reduce-scatter.2.cloned.1.call-update) | async-done | bytes 196624 | tf_op jit(solution)/shard_map/reduce_scatter | solution.py:59
  85.3 1.0 fusion.6
  86.3 0.1 copy.11
  86.4 0.1 copy.10
  86.6 1.5 %fusion = f32[24,64,64]{2,1,0:T(8,128)S(1)} fusion(f32[24,16,64]{2,1,0:T(8,128)S(1)} %bitcast.21, f32[24,16,64]{2,1,0:T(8,128)S(1)} %bitcast.22, f32[24,16]{1,0:T(8,128)S(1)} %fusion.5), kind=kOutput, calls=%fused_computation.4 | convolution fusion | flops 18898944 | bytes 591360 | tf_op jit(solution)/shard_map/qti,qtj->qij/dot_general | solution.py:28
  88.1 0.8 convolution_bitcast_fusion
  88.9 0.0 copy-done.4
  88.9 0.8 convolution_convert_fusion
  89.7 1.1 convert_element_type.15
  90.8 0.0 all-gather.2.cloned.1.call-update
  91.5 43.6 %all-gather.2.cloned.1.call-done = bf16[384,4096]{1,0:T(8,128)(2,1)} async-done(((bf16[24,4096]{1,0:T(8,128)(2,1)}), bf16[384,4096]{1,0:T(8,128)(2,1)}) %all-gather.2.cloned.1.call-update) | async-done | bytes 3145744 | tf_op jit(solution)/shard_map/all_gather | solution.py:67
  135.0 5.8 %convolution_select_fusion = f32[384,512]{1,0:T(8,128)} fusion(bf16[384,4096]{1,0:T(8,128)(2,1)} %all-gather.2.cloned.1.call-done, bf16[512,4096]{1,0:T(8,128)(2,1)} %param.16, pred[512]{0:T(512)(128)(4,1)S(1)} %iota_compare_fusion.1), kind=kOutput, calls=%fused_computation.2 | convolution fusion | flops 1610809344 | bytes 8126976 | tf_op jit(solution)/shard_map/dot_general | solution.py:37
  (6 shorter events, 0.0 us)
Async XLA Ops:
  6.5 0.8 copy-start
  6.5 5.8 %copy-start.2 = (bf16[512,64]{0,1:T(8,128)(2,1)S(1)}, bf16[512,64]{0,1:T(8,128)(2,1)}, u32[]{:S(2)}) copy-start(bf16[512,64]{0,1:T(8,128)(2,1)} %param.11) | copy-start | bytes 196612
  6.5 78.8 %reduce-scatter.2.cloned.1.call-start = ((), (), s32[]{:S(2)}) async-start(), calls=%async_computation.1 | async-start | bytes 3342336 | tf_op jit(solution)/shard_map/reduce_scatter | solution.py:59
  7.4 4.9 %copy-start.1 = (bf16[6144,512]{1,0:T(8,128)(2,1)S(1)}, bf16[6144,512]{1,0:T(8,128)(2,1)}, u32[]{:S(2)}) copy-start(bf16[6144,512]{1,0:T(8,128)(2,1)} %param.9) | copy-start | bytes 18874372
  16.2 71.9 %copy-start.3 = (f32[64,64]{1,0:T(8,128)S(1)}, f32[64,64]{1,0:T(8,128)}, u32[]{:S(2)}) copy-start(f32[64,64]{1,0:T(8,128)} %param.13) | copy-start | bytes 49156
  16.2 72.7 %copy-start.4 = (f32[64,64]{1,0:T(8,128)S(1)}, f32[64,64]{1,0:T(8,128)}, u32[]{:S(2)}) copy-start(f32[64,64]{1,0:T(8,128)} %param.14) | copy-start | bytes 49156
  16.2 118.8 %all-gather.2.cloned.1.call-start = ((), (), s32[]{:S(2)}) async-start(), calls=%async_computation.2 | async-start | bytes 3342336 | tf_op jit(solution)/shard_map/all_gather | solution.py:67
Sparse Core Ops, SparseCore 0:
  16.4 68.9 reduce-scatter.1
  90.9 44.0 all-gather.1
where the time goes:
time: 148 us
  waiting for transfers between devices  112 us (76%)
  matrix products  15.9 us (11%)
  between operations  14.1 us (10%)
  local copies, waits for them, and re-layouts  3.86 us (3%)
  other arithmetic  1.97 us (1%)
    reduce_scatter x1, waiting for transfers between devices, local(): lax.psum_scatter(project_pair(layer_input, output_grad, proj_in, proj_out...  68.2 us
    all_gather x1, waiting for transfers between devices, local(): lax.all_gather(query_grads, 'store', axis=0, tiled=True)  43.6 us
    dot_general x1, matrix products, score_block(): lax.dot_general(query_grads, store_rows, (((1,), (1,)), ((), ())), prefer...  5.85 us
    dot_general x1, matrix products, project_pair(): jnp.dot(grad_rows, weight_out, preferred_element_type=jnp.float32)  4.93 us
  transfers between devices with their start and end apart: 2, of which 2 were waited for; matrix products, arithmetic and copies ran while one was open for 1% of the time, Pallas kernels for 0%

commit v1 on v0

v1 whole, which is shorter than its diff:
```python
import functools

import jax
import jax.numpy as jnp
from jax import lax
from jax.experimental import pallas as pl
from jax.experimental.pallas import tpu as pltpu
from jax.sharding import PartitionSpec as P

STEPS = 512.0
LOW = 40.0
TOP = 32767.0
LOG2E = 1.4426950408889634
TINY = 1e-30
MESH_IDS = pl.DeviceIdType.MESH


def encode(values):
    size = jnp.log(jnp.maximum(jnp.abs(values), TINY)) * (LOG2E * STEPS) + LOW * STEPS
    size = jnp.clip(jnp.floor(size + 0.5), 0.0, TOP)
    return jnp.where(values < 0.0, -size, size).astype(jnp.int32).astype(jnp.int16)


def decode(codes):
    signed = codes.astype(jnp.int32).astype(jnp.float32)
    size = jnp.exp2(jnp.abs(signed) * (1.0 / STEPS) - LOW)
    return jnp.where(signed < 0.0, -size, jnp.where(signed > 0.0, size, 0.0))


def split_store(n):
    cores = 2 if n % 2 == 0 else 1
    rest = n // cores
    xs = 1
    while (2 * xs) ** 3 <= rest and rest % (2 * xs) == 0:
        xs *= 2
    return rest // xs, xs, cores


def pieces_of(rows, wanted):
    count = wanted
    while count > 1 and (rows % count or (rows // count) % 16):
        count -= 1
    return count


def reduce_kernel(
    zs, xs, cs, parts,
    in_hbm, out_hbm, w_in, w_out, full,
    in_rows, out_rows, wide, core_send, core_recv, own, x_send, x_recv, z_send, z_recv,
    load_sem, cs_sem, cr_sem, xs_sem, xr_sem, zs_sem, zr_sem,
    gz_s, gz_r, gx_s, gx_r, gc_s, gc_r,
):
    rank = w_in.shape[1]
    slab = own.shape[1]
    run = slab // zs
    me = lax.axis_index("store")
    c = lax.rem(me, cs)
    x = lax.rem(me // cs, xs)
    z = me // (cs * xs)

    def device(zz, xx, cc):
        return {"store": (zz * xs + xx) * cs + cc}

    def start_of(cc, xx, p):
        return pl.multiple_of(((cc * xs + xx) * parts + p) * slab, slab)

    x_of = [lax.rem(x + d, xs) for d in range(xs)]
    z_of = [lax.rem(z + d, zs) for d in range(zs)]
    core = 1 - c if cs == 2 else c

    order = []
    x_order = list(range(1, xs)) + [0]
    if cs == 2:
        order += [(1, d, p) for p in range(parts) for d in x_order]
    order += [(0, d, p) for p in range(parts) for d in x_order]
    loads = []
    for k, (side, d, p) in enumerate(order):
        rows = pl.ds(start_of(core if side else c, x_of[d], p), slab)
        pair = (
            pltpu.make_async_copy(in_hbm.at[rows], in_rows.at[k], load_sem.at[2 * k]),
            pltpu.make_async_copy(out_hbm.at[rows], out_rows.at[k], load_sem.at[2 * k + 1]),
        )
        for load in pair:
            load.start()
        loads.append(pair)

    barrier = pltpu.get_barrier_semaphore()
    partners = [device(z, x_of[d], c) for d in range(1, xs)]
    partners += [device(z_of[d], x, c) for d in range(1, zs)]
    if cs == 2:
        partners.append(device(z, x, core))
    for partner in partners:
        pl.semaphore_signal(barrier, inc=1, device_id=partner, device_id_type=MESH_IDS)

    wide[...] = jnp.zeros_like(wide)
    wide[0, :, :rank] = w_in[...]
    wide[1, :, rank:] = w_out[...]

    def project(k):
        for load in loads[k]:
            load.wait()
        return jnp.dot(
            in_rows[k], wide[0], preferred_element_type=jnp.float32
        ) + jnp.dot(out_rows[k], wide[1], preferred_element_type=jnp.float32)

    def send(src, dst, s_sem, r_sem, target):
        copy = pltpu.make_async_remote_copy(
            src_ref=src, dst_ref=dst, send_sem=s_sem, recv_sem=r_sem,
            device_id=target, device_id_type=MESH_IDS,
        )
        copy.start()
        return copy

    sent = []
    cores = {}
    first = True
    for k, (side, d, p) in enumerate(order):
        slot = p * xs + d
        if side:
            core_send[slot] = project(k)
            if first:
                pl.semaphore_wait(barrier, len(partners))
                first = False
            cores[slot] = send(
                core_send.at[slot], core_recv.at[slot], cs_sem.at[slot], cr_sem.at[slot],
                device(z, x, core),
            )
            sent.append(cores[slot])
    xcopies = {}
    for k, (side, d, p) in enumerate(order):
        if side:
            continue
        slot = p * xs + d
        total = project(k)
        if first:
            pl.semaphore_wait(barrier, len(partners))
            first = False
        if cs == 2:
            cores[slot].wait_recv()
            total = total + core_recv[slot]
        if d == 0:
            own[p] = total
        else:
            at = p * xs + d
            x_send[at] = encode(total)
            xcopies[p, d] = send(
                x_send.at[at], x_recv.at[at], xs_sem.at[at], xr_sem.at[at], device(z, x_of[d], c)
            )
            sent.append(xcopies[p, d])
    zcopies = {}
    for p in range(parts):
        total = own[p]
        for d in range(1, xs):
            xcopies[p, d].wait_recv()
            total = total + decode(x_recv[p * xs + d])
        own[p] = total
        z_send[p] = encode(total)
        for d in range(1, zs):
            at = p * zs + d
            zcopies[p, d] = send(
                z_send.at[p, pl.ds(pl.multiple_of(z_of[d] * run, run), run)],
                z_recv.at[at], zs_sem.at[at], zr_sem.at[at], device(z_of[d], x, c),
            )
            sent.append(zcopies[p, d])
    gz = {}
    for p in range(parts):
        total = own[p, pl.ds(pl.multiple_of(z * run, run), run), :]
        for d in range(1, zs):
            zcopies[p, d].wait_recv()
            total = total + decode(z_recv[p * zs + d])
        mine = pl.ds(pl.multiple_of(start_of(c, x, p) + z * run, run), run)
        full[mine, :] = encode(total)
        for d in range(1, zs):
            at = p * zs + d
            gz[p, d] = send(
                full.at[mine], full.at[mine], gz_s.at[at], gz_r.at[at], device(z_of[d], x, c)
            )
            sent.append(gz[p, d])
    gx = {}
    gc = {}
    for p in range(parts):
        for d in range(1, zs):
            gz[p, d].wait_recv()
        mine = pl.ds(start_of(c, x, p), slab)
        for d in range(1, xs):
            at = p * xs + d
            gx[p, d] = send(
                full.at[mine], full.at[mine], gx_s.at[at], gx_r.at[at], device(z, x_of[d], c)
            )
            sent.append(gx[p, d])
        if cs == 2:
            at = p * xs
            gc[at] = send(
                full.at[mine], full.at[mine], gc_s.at[at], gc_r.at[at], device(z, x, core)
            )
            sent.append(gc[at])
    for p in range(parts):
        for d in range(1, xs):
            gx[p, d].wait_recv()
            if cs == 2:
                at = p * xs + d
                came = pl.ds(start_of(c, lax.rem(x + xs - d, xs), p), slab)
                gc[at] = send(
                    full.at[came], full.at[came], gc_s.at[at], gc_r.at[at], device(z, x, core)
                )
                sent.append(gc[at])
    for copy in gc.values():
        copy.wait_recv()
    for copy in sent:
        copy.wait_send()


def reduced_factors(n, layer_input, output_grad, proj_in, proj_out):
    zs, xs, cs = split_store(n)
    tokens, depth = layer_input.shape
    width = 2 * proj_in.shape[1]
    parts = pieces_of(tokens // n, 2)
    slab = tokens // (cs * xs * parts)
    run = slab // zs
    slabs = cs * xs * parts
    dma = pltpu.SemaphoreType.DMA
    return pl.pallas_call(
        functools.partial(reduce_kernel, zs, xs, cs, parts),
        out_shape=jax.ShapeDtypeStruct((tokens, width), jnp.int16),
        in_specs=[pl.BlockSpec(memory_space=pl.ANY)] * 2
        + [pl.BlockSpec(memory_space=pltpu.VMEM)] * 2,
        out_specs=pl.BlockSpec(memory_space=pltpu.VMEM),
        scratch_shapes=[
            pltpu.VMEM((slabs, slab, depth), jnp.bfloat16),
            pltpu.VMEM((slabs, slab, depth), jnp.bfloat16),
            pltpu.VMEM((2, depth, width), jnp.bfloat16),
            pltpu.VMEM((parts * xs, slab, width), jnp.float32),
            pltpu.VMEM((parts * xs, slab, width), jnp.float32),
            pltpu.VMEM((parts, slab, width), jnp.float32),
            pltpu.VMEM((parts * xs, slab, width), jnp.int16),
            pltpu.VMEM((parts * xs, slab, width), jnp.int16),
            pltpu.VMEM((parts, slab, width), jnp.int16),
            pltpu.VMEM((parts * zs, run, width), jnp.int16),
            dma((2 * slabs,)),
            dma((parts * xs,)), dma((parts * xs,)),
            dma((parts * xs,)), dma((parts * xs,)),
            dma((parts * zs,)), dma((parts * zs,)),
            dma((parts * zs,)), dma((parts * zs,)),
            dma((parts * xs,)), dma((parts * xs,)),
            dma((parts * xs,)), dma((parts * xs,)),
        ],
        compiler_params=pltpu.CompilerParams(
            collective_id=0, has_side_effects=True, vmem_limit_bytes=48 * 1024 * 1024
        ),
        name="reduce_factors",
    )(layer_input, output_grad, proj_in, proj_out)


def halves(values):
    high = values.astype(jnp.bfloat16)
    return high, (values - high.astype(jnp.float32)).astype(jnp.bfloat16)


def score_kernel(
    query_len, factors, pin, pout, lengths, live, store_hbm, scores,
    store, grads, corner, store_sem,
):
    rank = pin.shape[0]
    width = 2 * rank
    queries = lengths.shape[0]
    group = 8
    tokens = group * query_len
    fetch = pltpu.make_async_copy(store_hbm, store, store_sem)
    fetch.start()

    corner[...] = jnp.zeros_like(corner)
    corner[:rank, :rank] = pin[...]
    flipped = corner[...].T
    corner[:rank, :rank] = jnp.zeros_like(pin)
    corner[rank:, rank:] = pout[...]
    w_high, w_low = halves(flipped + corner[...])
    weights = jnp.concatenate([w_high, w_low], axis=1)
    weights = jnp.concatenate([weights, weights], axis=0)

    lane = lax.broadcasted_iota(jnp.int32, (group, tokens), 1)
    row = lax.broadcasted_iota(jnp.int32, (group, tokens), 0)
    token = lane - row * query_len
    low_lane = lax.broadcasted_iota(jnp.int32, (1, 1, width), 2) < rank

    def one_group(first):
        part = decode(factors[pl.ds(first * query_len, tokens), :])
        high, low = halves(part)
        both = jnp.dot(
            jnp.concatenate([high, low], axis=1), weights, preferred_element_type=jnp.float32
        )
        done = both[:, :width] + both[:, width:]
        left = done.T[:rank]
        keep = (token >= 0) & (token < lengths[pl.ds(first, group), :])
        left_high = left.astype(jnp.bfloat16).astype(jnp.float32)
        left_low = left - left_high
        spread = [
            jnp.where(keep[None], side[:, None, :], 0.0)
            .reshape(rank * group, tokens)
            .astype(jnp.bfloat16)
            for side in (left_high, left_low)
        ]
        right = done[:, rank:]
        right_high, right_low = halves(jnp.concatenate([right, right], axis=1))
        column = jnp.concatenate([right_high, right_low], axis=1)
        outer = jnp.dot(
            jnp.concatenate(spread, axis=1),
            jnp.concatenate([column, column], axis=0),
            preferred_element_type=jnp.float32,
        )
        outer = (outer[:, :width] + outer[:, width:]).reshape(rank // 2, 2, group, width)
        return jnp.where(low_lane, outer[:, 0], outer[:, 1])

    def body(step, carry):
        first = pl.multiple_of(step * 2 * group, 2 * group)
        pair = jnp.concatenate([one_group(first), one_group(first + group)], axis=1)
        pair = pair.astype(jnp.bfloat16)
        for m in range(rank // 2):
            grads[pl.ds(first, 2 * group), m * width : (m + 1) * width] = pair[m]
        return carry

    lax.fori_loop(0, queries // (2 * group), body, 0)

    fetch.wait()
    tile = 256
    for at in range(0, store.shape[0], tile):
        products = lax.dot_general(
            grads[...], store[at : at + tile, :], (((1,), (1,)), ((), ())),
            preferred_element_type=jnp.float32,
        )
        index = lax.broadcasted_iota(jnp.int32, (1, tile), 1) + at
        scores[:, at : at + tile] = jnp.where(index < live[0], products, 0.0)


def score(factors, precond_in, precond_out, lengths, store_rows, store_live):
    queries = lengths.shape[0]
    query_len = factors.shape[0] // queries
    rank = precond_in.shape[0]
    rows, flat = store_rows.shape
    vmem = pl.BlockSpec(memory_space=pltpu.VMEM)
    return pl.pallas_call(
        functools.partial(score_kernel, query_len),
        out_shape=jax.ShapeDtypeStruct((queries, rows), jnp.float32),
        in_specs=[vmem, vmem, vmem, vmem, pl.BlockSpec(memory_space=pltpu.SMEM),
                  pl.BlockSpec(memory_space=pl.ANY)],
        out_specs=vmem,
        scratch_shapes=[
            pltpu.VMEM((rows, flat), jnp.bfloat16),
            pltpu.VMEM((queries, flat), jnp.bfloat16),
            pltpu.VMEM((2 * rank, 2 * rank), jnp.float32),
            pltpu.SemaphoreType.DMA,
        ],
        compiler_params=pltpu.CompilerParams(vmem_limit_bytes=48 * 1024 * 1024),
        name="score_store",
    )(factors, precond_in, precond_out, lengths[:, None], store_live, store_rows)


def solution(mesh):
    n = mesh.shape["store"]

    def local(
        layer_input, output_grad, proj_in, proj_out, precond_in, precond_out,
        query_lengths, store_rows, store_live,
    ):
        factors = reduced_factors(n, layer_input, output_grad, proj_in, proj_out)
        return score(factors, precond_in, precond_out, query_lengths, store_rows, store_live)

    placed = (
        P("groups", "store"),
        P("groups", "store"),
        P("store", None),
        P("store", None),
        P(),
        P(),
        P("groups"),
        P("store", None),
        P("store"),
    )
    return jax.shard_map(
        local, mesh=mesh, in_specs=placed, out_specs=P("groups", "store"), check_vma=False
    )
```

time: 148 us -> 61.3 us (0.41)
  waiting for transfers between devices: 112 us -> 0 us
  Pallas kernels: 0 us -> 57.5 us
  matrix products: 15.9 us -> 0 us
  between operations: 14.1 us -> 0.73 us
  other arithmetic: 1.97 us -> 0 us
    reduce_scatter x1 -> x0, waiting for transfers between devices: 68.2 us -> none  [local(): lax.psum_scatter(project_pair(layer_input, output_grad, proj_in, proj_out...]
    pallas_call x0 -> x2, Pallas kernels: none -> 57.5 us  [the longest x1 40.6 us: reduced_factors(): pl.pallas_call(functools.partial(reduce_kernel, zs, xs, cs, parts), out_s...]
    all_gather x1 -> x0, waiting for transfers between devices: 43.6 us -> none  [local(): lax.all_gather(query_grads, 'store', axis=0, tiled=True)]
    dot_general x6 -> x0, matrix products: 15.9 us -> none  [the longest x1 5.85 us: score_block(): lax.dot_general(query_grads, store_rows, (((1,), (1,)), ((), ())), prefer...]
    concatenate x1 -> x0, other arithmetic: 1.89 us -> none  [project_pair(): jnp.concatenate([jnp.dot(input_rows, weight_in, preferred_element_type=jn...]
  transfers between devices with their start and end apart: 2 -> 0, of which waited for: 2 -> 0; matrix products, arithmetic and copies ran while one was open for 1% -> 0% of each run, Pallas kernels for 0% -> 0%
where the time goes in v1:
time: 61.3 us; the launch traced here: 60.9 us
  Pallas kernels  57.5 us (94%)
  local copies, waits for them, and re-layouts  2.73 us (4%)
  between operations  0.73 us (1%)
    pallas_call x1, Pallas kernels, reduced_factors(): pl.pallas_call(functools.partial(reduce_kernel, zs, xs, cs, parts), out_s...  40.6 us
    pallas_call x1, Pallas kernels, score(): pl.pallas_call(functools.partial(score_kernel, query_len), out_shape=jax....  16.9 us
    unnamed x8, local copies, waits for them, and re-layouts  1.93 us

profile of v1, /device:TPU:0, one launch (start us, length us, event | category | flops | bytes accessed | tf_op | source)
XLA Modules:
  0.0 60.9 jit_solution(12746987957609662122)
XLA Ops:
  0.7 1.0 %copy.12.w_in = bf16[512,64]{1,0:T(8,128)(2,1)S(1)} copy(bf16[512,64]{0,1:T(8,128)(2,1)} %param.11) | data formatting | bytes 131072 | tf_op args[2]
  1.6 1.0 %copy.13.w_out = bf16[512,64]{1,0:T(8,128)(2,1)S(1)} copy(bf16[512,64]{0,1:T(8,128)(2,1)} %param.12) | data formatting | bytes 131072 | tf_op args[3]
  2.6 0.8 %broadcast_in_dim.4.lengths = s32[384,1]{1,0:T(8,128)S(1)} reshape(s32[384]{0:T(512)} %param.15) | data formatting | bytes 3072 | tf_op jit(solution)/shard_map/broadcast_in_dim | solution.py:354
  3.4 0.0 copy-start
  3.4 0.0 copy-start.1
  3.4 0.0 copy-start.2
  3.4 40.6 %reduce_factors.1.factors = s16[6144,128]{1,0:T(8,128)(2,1)S(1)} custom-call(bf16[6144,512]{1,0:T(8,128)(2,1)} %in_hbm.1, bf16[6144,512]{1,0:T(8,128)(2,1)} %out_hbm.1, bf16[512,64]{1,0:T(8,128)(2,1)S(1)} %copy.12.w_in, bf16[512,64]{1,0:T(8,128)(2,1)S(1)} %copy.13.w_out), custom_call_target="tpu_custom_call" | custom-call | tf_op jit(solution)/shard_map/reduce_factors/pallas_call | solution.py:222
  44.0 0.0 copy-done
  44.0 0.0 copy-done.1
  44.0 0.0 copy-done.2
  44.0 16.9 %score_store.1 = f32[384,512]{1,0:T(8,128)} custom-call(s16[6144,128]{1,0:T(8,128)(2,1)S(1)} %reduce_factors.1.factors, f32[64,64]{1,0:T(8,128)S(1)} %copy-done.1, f32[64,64]{1,0:T(8,128)S(1)} %copy-done.2, s32[384,1]{1,0:T(8,128)S(1)} %broadcast_in_dim.4.lengths, s32[1]{0:T(128)S(6)} %copy.15.live, bf16[512,4096]{1,0:T(8,128)(2,1)S(1)} %copy-done), custom_call_target="tpu_custom_call" | custom-call | tf_op jit(solution)/shard_map/score_store/pallas_call | solution.py:340
Async XLA Ops:
  3.4 40.6 %copy-start = (bf16[512,4096]{1,0:T(8,128)(2,1)S(1)}, bf16[512,4096]{1,0:T(8,128)(2,1)}, u32[]{:S(2)}) copy-start(bf16[512,4096]{1,0:T(8,128)(2,1)} %store_hbm.1) | copy-start | bytes 12582916
  3.4 40.6 %copy-start.1 = (f32[64,64]{1,0:T(8,128)S(1)}, f32[64,64]{1,0:T(8,128)}, u32[]{:S(2)}) copy-start(f32[64,64]{1,0:T(8,128)} %pin.1) | copy-start | bytes 49156
  3.4 40.6 %copy-start.2 = (f32[64,64]{1,0:T(8,128)S(1)}, f32[64,64]{1,0:T(8,128)}, u32[]{:S(2)}) copy-start(f32[64,64]{1,0:T(8,128)} %pout.1) | copy-start | bytes 49156

commit v2 on v1

v2 whole, which is shorter than its diff:
```python
import functools

import jax
import jax.numpy as jnp
from jax import lax
from jax.experimental import pallas as pl
from jax.experimental.pallas import tpu as pltpu
from jax.sharding import PartitionSpec as P

STEPS = 512.0
LOW = 40.0
TOP = 32767.0
LOG2E = 1.4426950408889634
TINY = 1e-30
MESH_IDS = pl.DeviceIdType.MESH
NT = (((1,), (1,)), ((), ()))
PARTS = 3


def encode(values):
    size = jnp.log(jnp.maximum(jnp.abs(values), TINY)) * (LOG2E * STEPS) + LOW * STEPS
    size = jnp.clip(jnp.floor(size + 0.5), 0.0, TOP)
    return jnp.where(values < 0.0, -size, size).astype(jnp.int32).astype(jnp.int16)


def decode(codes):
    signed = codes.astype(jnp.int32).astype(jnp.float32)
    size = jnp.exp2(jnp.abs(signed) * (1.0 / STEPS) - LOW)
    return jnp.where(signed < 0.0, -size, jnp.where(signed > 0.0, size, 0.0))


def split_store(n):
    cores = 2 if n % 2 == 0 else 1
    rest = n // cores
    xs = 1
    while (2 * xs) ** 3 <= rest and rest % (2 * xs) == 0:
        xs *= 2
    return rest // xs, xs, cores


def pieces_of(rows, slab, block, wanted):
    count = wanted
    while count > 1 and (rows % count or (rows // count) % 16 or (slab // count) % block):
        count -= 1
    return count


def halves(values):
    high = values.astype(jnp.bfloat16)
    return high, (values - high.astype(jnp.float32)).astype(jnp.bfloat16)


def lanes_to_rows(row, lanes):
    return jnp.broadcast_to(row, (lanes, lanes)).T


def attribution_kernel(
    zs, xs, cs, parts, query_len,
    in_hbm, out_hbm, w_in, w_out, pin, pout, lengths, live, store_hbm, scores,
    full, store, grads, corner, counted, weights, left_parts, right_parts, store_sem,
    in_rows, out_rows, wide, core_send, core_recv, own, x_send, x_recv, z_send, z_recv,
    load_sem, cs_sem, cr_sem, xs_sem, xr_sem, zs_sem, zr_sem,
    gz_s, gz_r, gx_s, gx_r, gc_s, gc_r,
):
    rank = w_in.shape[0]
    width = 2 * rank
    group = 8
    tokens = group * query_len
    slab = own.shape[1]
    run = slab // zs
    me = lax.axis_index("store")
    c = lax.rem(me, cs)
    x = lax.rem(me // cs, xs)
    z = me // (cs * xs)

    def device(zz, xx, cc):
        return {"store": (zz * xs + xx) * cs + cc}

    def start_of(cc, xx, p):
        return pl.multiple_of(((cc * xs + xx) * parts + p) * slab, slab)

    x_of = [lax.rem(x + d, xs) for d in range(xs)]
    z_of = [lax.rem(z + d, zs) for d in range(zs)]
    core = 1 - c if cs == 2 else c

    order = []
    x_order = list(range(1, xs)) + [0]
    if cs == 2:
        order += [(1, d, p) for p in range(parts) for d in x_order]
    order += [(0, d, p) for p in range(parts) for d in x_order]
    loads = []
    for k, (side, d, p) in enumerate(order):
        rows = pl.ds(start_of(core if side else c, x_of[d], p), slab)
        pair = (
            pltpu.make_async_copy(in_hbm.at[rows], in_rows.at[k], load_sem.at[2 * k]),
            pltpu.make_async_copy(out_hbm.at[rows], out_rows.at[k], load_sem.at[2 * k + 1]),
        )
        for load in pair:
            load.start()
        loads.append(pair)

    fetch = pltpu.make_async_copy(store_hbm, store, store_sem)
    fetch.start()

    barrier = pltpu.get_barrier_semaphore()
    partners = [device(z, x_of[d], c) for d in range(1, xs)]
    partners += [device(z_of[d], x, c) for d in range(1, zs)]
    if cs == 2:
        partners.append(device(z, x, core))
    for partner in partners:
        pl.semaphore_signal(barrier, inc=1, device_id=partner, device_id_type=MESH_IDS)

    wide[...] = jnp.zeros_like(wide)
    wide[0, :rank, :] = w_in[...]
    wide[1, rank:, :] = w_out[...]

    def project(k):
        for load in loads[k]:
            load.wait()
        return lax.dot_general(
            in_rows[k], wide[0], NT, preferred_element_type=jnp.float32
        ) + lax.dot_general(out_rows[k], wide[1], NT, preferred_element_type=jnp.float32)

    def send(src, dst, s_sem, r_sem, target):
        copy = pltpu.make_async_remote_copy(
            src_ref=src, dst_ref=dst, send_sem=s_sem, recv_sem=r_sem,
            device_id=target, device_id_type=MESH_IDS,
        )
        copy.start()
        return copy

    sent = []
    cores = {}
    first = True
    for k, (side, d, p) in enumerate(order):
        slot = p * xs + d
        if side:
            core_send[slot] = project(k)
            if first:
                pl.semaphore_wait(barrier, len(partners))
                first = False
            cores[slot] = send(
                core_send.at[slot], core_recv.at[slot], cs_sem.at[slot], cr_sem.at[slot],
                device(z, x, core),
            )
            sent.append(cores[slot])
    xcopies = {}
    for k, (side, d, p) in enumerate(order):
        if side:
            continue
        slot = p * xs + d
        total = project(k)
        if first:
            pl.semaphore_wait(barrier, len(partners))
            first = False
        if cs == 2:
            cores[slot].wait_recv()
            total = total + core_recv[slot]
        if d == 0:
            own[p] = total
        else:
            at = p * xs + d
            x_send[at] = encode(total)
            xcopies[p, d] = send(
                x_send.at[at], x_recv.at[at], xs_sem.at[at], xr_sem.at[at], device(z, x_of[d], c)
            )
            sent.append(xcopies[p, d])
    corner[...] = jnp.zeros_like(corner)
    corner[:rank, :rank] = pin[...]
    flipped = corner[...].T
    corner[:rank, :rank] = jnp.zeros_like(pin)
    corner[rank:, rank:] = pout[...]
    w_high, w_low = halves(flipped + corner[...])
    both_weights = jnp.concatenate([w_high, w_low], axis=1)
    weights[...] = jnp.concatenate([both_weights, both_weights], axis=0)
    for at in range(0, lengths.shape[1], width):
        counted[at : at + width, :] = lanes_to_rows(
            lengths[:, at : at + width].astype(jnp.float32), width
        )

    zcopies = {}
    for p in range(parts):
        total = own[p]
        for d in range(1, xs):
            xcopies[p, d].wait_recv()
            total = total + decode(x_recv[p * xs + d])
        own[p] = total
        z_send[p] = encode(total)
        for d in range(1, zs):
            at = p * zs + d
            zcopies[p, d] = send(
                z_send.at[p, pl.ds(pl.multiple_of(z_of[d] * run, run), run)],
                z_recv.at[at], zs_sem.at[at], zr_sem.at[at], device(z_of[d], x, c),
            )
            sent.append(zcopies[p, d])
    gz = {}
    for p in range(parts):
        total = own[p, pl.ds(pl.multiple_of(z * run, run), run), :]
        for d in range(1, zs):
            zcopies[p, d].wait_recv()
            total = total + decode(z_recv[p * zs + d])
        mine = pl.ds(pl.multiple_of(start_of(c, x, p) + z * run, run), run)
        full[mine, :] = encode(total)
        for d in range(1, zs):
            at = p * zs + d
            gz[p, d] = send(
                full.at[mine], full.at[mine], gz_s.at[at], gz_r.at[at], device(z_of[d], x, c)
            )
            sent.append(gz[p, d])
    lane = lax.broadcasted_iota(jnp.int32, (group, tokens), 1)
    row = lax.broadcasted_iota(jnp.int32, (group, tokens), 0)
    token = lane - row * query_len
    own_tokens = token >= 0
    token = token.astype(jnp.float32)
    low_lane = lax.broadcasted_iota(jnp.int32, (1, 1, width), 2) < rank

    def one_group(k, first_query):
        keep = own_tokens & (token < counted[pl.ds(first_query, group), :])
        spread = [
            jnp.where(keep[None], left_parts[half, k][:, None, :], 0.0)
            .reshape(rank * group, tokens)
            .astype(jnp.bfloat16)
            for half in range(2)
        ]
        column = right_parts[pl.ds(pl.multiple_of(k * tokens, tokens), tokens), :]
        outer = jnp.dot(
            jnp.concatenate(spread, axis=1),
            jnp.concatenate([column, column], axis=0),
            preferred_element_type=jnp.float32,
        )
        outer = (outer[:, :width] + outer[:, width:]).reshape(rank // 2, 2, group, width)
        return jnp.where(low_lane, outer[:, 0], outer[:, 1])

    def grads_of(start):
        high, low = halves(decode(full[pl.ds(start, slab), :]))
        both = jnp.dot(
            jnp.concatenate([high, low], axis=1), weights[...], preferred_element_type=jnp.float32
        )
        done = both[:, :width] + both[:, width:]
        for k in range(slab // tokens):
            left = done[k * tokens : (k + 1) * tokens].T[:rank]
            left_high = left.astype(jnp.bfloat16).astype(jnp.float32)
            left_parts[0, k] = left_high
            left_parts[1, k] = left - left_high
        right = done[:, rank:]
        right_high, right_low = halves(jnp.concatenate([right, right], axis=1))
        right_parts[...] = jnp.concatenate([right_high, right_low], axis=1)

        def body(step, carry):
            first = pl.multiple_of(start // query_len + step * 2 * group, 2 * group)
            pair = jnp.concatenate(
                [one_group(2 * step, first), one_group(2 * step + 1, first + group)], axis=1
            ).astype(jnp.bfloat16)
            for m in range(rank // 2):
                grads[pl.ds(first, 2 * group), m * width : (m + 1) * width] = pair[m]
            return carry

        lax.fori_loop(0, slab // (2 * tokens), body, 0)

    gx = {}
    gc = {}
    for p in range(parts):
        for d in range(1, zs):
            gz[p, d].wait_recv()
        mine = pl.ds(start_of(c, x, p), slab)
        for d in range(1, xs):
            at = p * xs + d
            gx[p, d] = send(
                full.at[mine], full.at[mine], gx_s.at[at], gx_r.at[at], device(z, x_of[d], c)
            )
            sent.append(gx[p, d])
        if cs == 2:
            at = p * xs
            gc[at] = send(
                full.at[mine], full.at[mine], gc_s.at[at], gc_r.at[at], device(z, x, core)
            )
            sent.append(gc[at])
        grads_of(start_of(c, x, p))
    x_from = [lax.rem(x + xs - d, xs) for d in range(xs)]
    for p in range(parts):
        if cs == 2:
            gc[p * xs].wait_recv()
            grads_of(start_of(core, x, p))
        for d in range(1, xs):
            gx[p, d].wait_recv()
            if cs == 2:
                at = p * xs + d
                came = pl.ds(start_of(c, x_from[d], p), slab)
                gc[at] = send(
                    full.at[came], full.at[came], gc_s.at[at], gc_r.at[at], device(z, x, core)
                )
                sent.append(gc[at])
    for p in range(parts):
        for d in range(1, xs):
            grads_of(start_of(c, x_from[d], p))
            if cs == 2:
                gc[p * xs + d].wait_recv()
                grads_of(start_of(core, x_from[d], p))

    fetch.wait()
    tile = 256
    for at in range(0, store.shape[0], tile):
        products = lax.dot_general(
            grads[...], store[at : at + tile, :], NT, preferred_element_type=jnp.float32
        )
        index = lax.broadcasted_iota(jnp.int32, (1, tile), 1) + at
        scores[:, at : at + tile] = jnp.where(index < live[0], products, 0.0)
    for copy in sent:
        copy.wait_send()


def attribution(
    n, layer_input, output_grad, proj_in, proj_out, precond_in, precond_out, lengths, store_rows,
    store_live,
):
    zs, xs, cs = split_store(n)
    tokens, depth = layer_input.shape
    rank = proj_in.shape[1]
    width = 2 * rank
    queries = lengths.shape[0]
    query_len = tokens // queries
    rows, flat = store_rows.shape
    parts = pieces_of(tokens // n, tokens // (cs * xs), 16 * query_len, PARTS)
    slab = tokens // (cs * xs * parts)
    run = slab // zs
    slabs = cs * xs * parts
    group = 8 * query_len
    dma = pltpu.SemaphoreType.DMA
    vmem = pl.BlockSpec(memory_space=pltpu.VMEM)
    hbm = pl.BlockSpec(memory_space=pl.ANY)
    return pl.pallas_call(
        functools.partial(attribution_kernel, zs, xs, cs, parts, query_len),
        out_shape=jax.ShapeDtypeStruct((queries, rows), jnp.float32),
        in_specs=[hbm, hbm, vmem, vmem, vmem, vmem, vmem,
                  pl.BlockSpec(memory_space=pltpu.SMEM), hbm],
        out_specs=vmem,
        scratch_shapes=[
            pltpu.VMEM((tokens, width), jnp.int16),
            pltpu.VMEM((rows, flat), jnp.bfloat16),
            pltpu.VMEM((queries, flat), jnp.bfloat16),
            pltpu.VMEM((width, width), jnp.float32),
            pltpu.VMEM((queries, width), jnp.float32),
            pltpu.VMEM((2 * width, 2 * width), jnp.bfloat16),
            pltpu.VMEM((2, slab // group, rank, group), jnp.float32),
            pltpu.VMEM((slab, 2 * width), jnp.bfloat16),
            pltpu.SemaphoreType.DMA,
            pltpu.VMEM((slabs, slab, depth), jnp.bfloat16),
            pltpu.VMEM((slabs, slab, depth), jnp.bfloat16),
            pltpu.VMEM((2, width, depth), jnp.bfloat16),
            pltpu.VMEM((parts * xs, slab, width), jnp.float32),
            pltpu.VMEM((parts * xs, slab, width), jnp.float32),
            pltpu.VMEM((parts, slab, width), jnp.float32),
            pltpu.VMEM((parts * xs, slab, width), jnp.int16),
            pltpu.VMEM((parts * xs, slab, width), jnp.int16),
            pltpu.VMEM((parts, slab, width), jnp.int16),
            pltpu.VMEM((parts * zs, run, width), jnp.int16),
            dma((2 * slabs,)),
            dma((parts * xs,)), dma((parts * xs,)),
            dma((parts * xs,)), dma((parts * xs,)),
            dma((parts * zs,)), dma((parts * zs,)),
            dma((parts * zs,)), dma((parts * zs,)),
            dma((parts * xs,)), dma((parts * xs,)),
            dma((parts * xs,)), dma((parts * xs,)),
        ],
        compiler_params=pltpu.CompilerParams(
            collective_id=0, has_side_effects=True, vmem_limit_bytes=56 * 1024 * 1024
        ),
        name="attribution",
    )(
        layer_input, output_grad, proj_in.T, proj_out.T, precond_in, precond_out,
        lengths[None, :], store_live, store_rows,
    )


def solution(mesh):
    n = mesh.shape["store"]

    def local(
        layer_input, output_grad, proj_in, proj_out, precond_in, precond_out,
        query_lengths, store_rows, store_live,
    ):
        return attribution(
            n, layer_input, output_grad, proj_in, proj_out, precond_in, precond_out,
            query_lengths, store_rows, store_live,
        )

    placed = (
        P("groups", "store"),
        P("groups", "store"),
        P("store", None),
        P("store", None),
        P(),
        P(),
        P("groups"),
        P("store", None),
        P("store"),
    )
    return jax.shard_map(
        local, mesh=mesh, in_specs=placed, out_specs=P("groups", "store"), check_vma=False
    )
```

time: 61.3 us -> 53.2 us (0.87)
  Pallas kernels: 57.5 us -> 49 us
    pallas_call x2 -> x1, Pallas kernels: 57.5 us -> 49 us  [attribution(): pl.pallas_call(functools.partial(attribution_kernel, zs, xs, cs, parts, q...]
    unnamed x8 -> x1, local copies, waits for them, and re-layouts: 1.93 us -> 2.06 us
where the time goes in v2:
time: 53.2 us; the launch traced here: 52.9 us
  Pallas kernels  49 us (92%)
  local copies, waits for them, and re-layouts  3.31 us (6%)
  between operations  0.66 us (1%)
    pallas_call x1, Pallas kernels, attribution(): pl.pallas_call(functools.partial(attribution_kernel, zs, xs, cs, parts, q...  49 us
    unnamed x1, local copies, waits for them, and re-layouts  2.06 us
    broadcast_in_dim x1, local copies, waits for them, and re-layouts, attribution(): lengths[None, :]  1.25 us

profile of v2, /device:TPU:0, one launch (start us, length us, event | category | flops | bytes accessed | tf_op | source)
XLA Modules:
  0.0 52.9 jit_solution(8996035553312331454)
XLA Ops:
  0.7 1.2 %broadcast_in_dim.3.lengths = s32[1,384]{1,0:T(1,128)} reshape(s32[384]{0:T(512)} %param.15) | data formatting | bytes 3072 | tf_op jit(solution)/shard_map/broadcast_in_dim | solution.py:371
  1.9 49.0 %attribution.1 = f32[384,512]{1,0:T(8,128)} custom-call(bf16[6144,512]{1,0:T(8,128)(2,1)} %in_hbm.1, bf16[6144,512]{1,0:T(8,128)(2,1)} %out_hbm.1, bf16[64,512]{1,0:T(8,128)(2,1)} %bitcast.2, bf16[64,512]{1,0:T(8,128)(2,1)} %bitcast.3, f32[64,64]{1,0:T(8,128)} %pin.1, f32[64,64]{1,0:T(8,128)} %pout.1, s32[1,384]{1,0:T(1,128)} %broadcast_in_dim.3.lengths, ...), custom_call_target="tpu_custom_call" | custom-call | tf_op jit(solution)/shard_map/attribution/pallas_call | solution.py:331
  50.9 2.1 %copy.12 = f32[384,512]{1,0:T(8,128)} copy(f32[384,512]{1,0:T(8,128)} %attribution.1) | data formatting | bytes 1572864

commit v3 on v2

--- a/solution.py
+++ b/solution.py
@@ -85,9 +85,11 @@
 
     order = []
     x_order = list(range(1, xs)) + [0]
-    if cs == 2:
-        order += [(1, d, p) for p in range(parts) for d in x_order]
-    order += [(0, d, p) for p in range(parts) for d in x_order]
+    for step in range(parts + 1):
+        if cs == 2 and step < parts:
+            order += [(1, d, step) for d in x_order]
+        if step > 0:
+            order += [(0, d, step - 1) for d in x_order]
     loads = []
     for k, (side, d, p) in enumerate(order):
         rows = pl.ds(start_of(core if side else c, x_of[d], p), slab)
@@ -129,42 +131,6 @@
         copy.start()
         return copy
 
-    sent = []
-    cores = {}
-    first = True
-    for k, (side, d, p) in enumerate(order):
-        slot = p * xs + d
-        if side:
-            core_send[slot] = project(k)
-            if first:
-                pl.semaphore_wait(barrier, len(partners))
-                first = False
-            cores[slot] = send(
-                core_send.at[slot], core_recv.at[slot], cs_sem.at[slot], cr_sem.at[slot],
-                device(z, x, core),
-            )
-            sent.append(cores[slot])
-    xcopies = {}
-    for k, (side, d, p) in enumerate(order):
-        if side:
-            continue
-        slot = p * xs + d
-        total = project(k)
-        if first:
-            pl.semaphore_wait(barrier, len(partners))
-            first = False
-        if cs == 2:
-            cores[slot].wait_recv()
-            total = total + core_recv[slot]
-        if d == 0:
-            own[p] = total
-        else:
-            at = p * xs + d
-            x_send[at] = encode(total)
-            xcopies[p, d] = send(
-                x_send.at[at], x_recv.at[at], xs_sem.at[at], xr_sem.at[at], device(z, x_of[d], c)
-            )
-            sent.append(xcopies[p, d])
     corner[...] = jnp.zeros_like(corner)
     corner[:rank, :rank] = pin[...]
     flipped = corner[...].T
@@ -178,8 +144,42 @@
             lengths[:, at : at + width].astype(jnp.float32), width
         )
 
+    sent = []
+    cores = {}
+    xcopies = {}
     zcopies = {}
-    for p in range(parts):
+    gz = {}
+    gx = {}
+    gc = {}
+
+    def to_core(p):
+        for d in x_order:
+            slot = p * xs + d
+            core_send[slot] = project(order.index((1, d, p)))
+            cores[slot] = send(
+                core_send.at[slot], core_recv.at[slot], cs_sem.at[slot], cr_sem.at[slot],
+                device(z, x, core),
+            )
+            sent.append(cores[slot])
+
+    def to_x(p):
+        for d in x_order:
+            at = p * xs + d
+            total = project(order.index((0, d, p)))
+            if cs == 2:
+                cores[at].wait_recv()
+                total = total + core_recv[at]
+            if d == 0:
+                own[p] = total
+            else:
+                x_send[at] = encode(total)
+                xcopies[p, d] = send(
+                    x_send.at[at], x_recv.at[at], xs_sem.at[at], xr_sem.at[at],
+                    device(z, x_of[d], c),
+                )
+                sent.append(xcopies[p, d])
+
+    def to_z(p):
         total = own[p]
         for d in range(1, xs):
             xcopies[p, d].wait_recv()
@@ -193,8 +193,8 @@
                 z_recv.at[at], zs_sem.at[at], zr_sem.at[at], device(z_of[d], x, c),
             )
             sent.append(zcopies[p, d])
-    gz = {}
-    for p in range(parts):
+
+    def back_z(p):
         total = own[p, pl.ds(pl.multiple_of(z * run, run), run), :]
         for d in range(1, zs):
             zcopies[p, d].wait_recv()
@@ -207,6 +207,7 @@
                 full.at[mine], full.at[mine], gz_s.at[at], gz_r.at[at], device(z_of[d], x, c)
             )
             sent.append(gz[p, d])
+
     lane = lax.broadcasted_iota(jnp.int32, (group, tokens), 1)
     row = lax.broadcasted_iota(jnp.int32, (group, tokens), 0)
     token = lane - row * query_len
@@ -257,9 +258,7 @@
 
         lax.fori_loop(0, slab // (2 * tokens), body, 0)
 
-    gx = {}
-    gc = {}
-    for p in range(parts):
+    def back_x(p):
         for d in range(1, zs):
             gz[p, d].wait_recv()
         mine = pl.ds(start_of(c, x, p), slab)
@@ -276,6 +275,13 @@
             )
             sent.append(gc[at])
         grads_of(start_of(c, x, p))
+
+    levels = ([to_core] if cs == 2 else []) + [to_x, to_z, back_z, back_x]
+    pl.semaphore_wait(barrier, len(partners))
+    for step in range(parts + len(levels) - 1):
+        for level, act in enumerate(levels):
+            if 0 <= step - level < parts:
+                act(step - level)
     x_from = [lax.rem(x + xs - d, xs) for d in range(xs)]
     for p in range(parts):
         if cs == 2:

time: 53.2 us -> 52.8 us (level)
  no operation moved by 1% of the time
where the time goes in v3:
time: 52.8 us; the launch traced here: 52.6 us
  Pallas kernels  48.6 us (92%)
  local copies, waits for them, and re-layouts  3.31 us (6%)
  between operations  0.66 us (1%)
    pallas_call x1, Pallas kernels, attribution(): pl.pallas_call(functools.partial(attribution_kernel, zs, xs, cs, parts, q...  48.6 us
    unnamed x1, local copies, waits for them, and re-layouts  2.06 us
    broadcast_in_dim x1, local copies, waits for them, and re-layouts, attribution(): lengths[None, :]  1.25 us

profile of v3, /device:TPU:0, one launch (start us, length us, event | category | flops | bytes accessed | tf_op | source)
XLA Modules:
  0.0 52.6 jit_solution(10326877622728049272)
XLA Ops:
  0.7 1.2 %broadcast_in_dim.3.lengths = s32[1,384]{1,0:T(1,128)} reshape(s32[384]{0:T(512)} %param.15) | data formatting | bytes 3072 | tf_op jit(solution)/shard_map/broadcast_in_dim | solution.py:377
  1.9 48.6 %attribution.1 = f32[384,512]{1,0:T(8,128)} custom-call(bf16[6144,512]{1,0:T(8,128)(2,1)} %in_hbm.1, bf16[6144,512]{1,0:T(8,128)(2,1)} %out_hbm.1, bf16[64,512]{1,0:T(8,128)(2,1)} %bitcast.2, bf16[64,512]{1,0:T(8,128)(2,1)} %bitcast.3, f32[64,64]{1,0:T(8,128)} %pin.1, f32[64,64]{1,0:T(8,128)} %pout.1, s32[1,384]{1,0:T(1,128)} %broadcast_in_dim.3.lengths, ...), custom_call_target="tpu_custom_call" | custom-call | tf_op jit(solution)/shard_map/attribution/pallas_call | solution.py:337
  50.5 2.1 %copy.12 = f32[384,512]{1,0:T(8,128)} copy(f32[384,512]{1,0:T(8,128)} %attribution.1) | data formatting | bytes 1572864
